TPU v7x, 512 devices: a whole 4x4x16 slice. The times are simulated.
512 devices in a mesh: day: 64 (over z, y), pair: 8 (over x, core).
Axes of the slice: x: 4, y: 4, z: 16, core: 2. Of those that a mesh axis runs over, the one named last changes fastest.
Arguments:
- spectra: bfloat16 [128, 128, 4096], P('day', 'pair'), may hold values from -40 to 40
- pair_stations: int32 [512, 2], P('pair'), may hold values from 0 to 127
- availability: int32 [128, 128], P('day'), may hold values from 0 to 1
Outputs:
- stacks: bfloat16 [128, 512, 1001], P('day', 'pair')
- reference: float32 [512, 1001], P('pair')
All inputs are finite; a program needn't handle non-finite values.
Results may differ from a plain program's by a relative error of at most 0.008.
Values may be sent and summed in bfloat16 or wider, within the bound.
A program may use at most 64 MiB of HBM per device.

v0:
```python
import jax
import jax.numpy as jnp
import numpy as np
from jax import lax
from jax.sharding import PartitionSpec as P

LAGS = 1001
WIDE = 1024
WINDOW = 30


def lag_table(bin_count):
    bin_ids = np.arange(bin_count)[:, None]
    lag_ids = np.arange(LAGS)[None, :] - (LAGS - 1) // 2
    angle = np.mod(bin_ids * lag_ids, 2 * bin_count) * (np.pi / bin_count)
    factor = 1.0 / np.sqrt(2.0 * bin_count)
    table = np.concatenate([np.cos(angle) * factor, -np.sin(angle) * factor], 0)
    return np.pad(table, ((0, 0), (0, WIDE - LAGS))).astype(np.float32).astype(jnp.bfloat16)


def per_device(spectra, pair_stations, availability):
    days_here = spectra.shape[0]
    groups = lax.axis_size("day")
    station_count = spectra.shape[1] * lax.axis_size("pair")
    bin_count = spectra.shape[2] // 2
    pairs_here = pair_stations.shape[0]
    inverse = jnp.asarray(lag_table(bin_count))
    station_ids = jnp.arange(station_count, dtype=jnp.int32)
    ends = jnp.concatenate([pair_stations[:, 0], pair_stations[:, 1]], 0)
    pick = (ends[:, None] == station_ids[None, :]).astype(jnp.bfloat16)
    avail = jnp.dot(availability.astype(jnp.bfloat16), pick.T, preferred_element_type=jnp.float32)
    present = avail[:, :pairs_here] * avail[:, pairs_here:]
    gathered = lax.all_gather(spectra, "pair", axis=1, tiled=True)
    rows = []
    for day in range(days_here):
        spec = jnp.dot(pick, gathered[day], preferred_element_type=jnp.float32)
        one, two = (spec[:pairs_here], spec[pairs_here:])
        ar, ai, br, bi = (
            one[:, :bin_count],
            one[:, bin_count:],
            two[:, :bin_count],
            two[:, bin_count:],
        )
        rows.append(jnp.concatenate([ar * br + ai * bi, ar * bi - ai * br], 1).astype(jnp.bfloat16))
    cross = jnp.concatenate(rows, 0)
    corr = jnp.dot(cross, inverse, preferred_element_type=jnp.float32)
    column = lax.broadcasted_iota(jnp.int32, (1, WIDE), 1)
    shown = present.reshape(-1, 1)
    daily = jnp.where(column == LAGS, shown, corr * shown).astype(jnp.bfloat16)
    daily = daily.reshape(days_here, pairs_here, WIDE)
    turned = lax.all_to_all(daily, "day", split_axis=1, concat_axis=0, tiled=True)
    days = groups * days_here
    mine = turned.reshape(days, WIDE)
    day_ids = np.arange(days)
    gap = day_ids[:, None] - day_ids[None, :]
    band = jnp.asarray(((gap >= 0) & (gap < WINDOW)).astype(np.float32), dtype=jnp.bfloat16)
    moving = jnp.dot(band, mine, preferred_element_type=jnp.float32)
    counts = moving[:, LAGS : LAGS + 1]
    ref = jnp.sum(mine.astype(jnp.float32), axis=0) / days
    ref = jnp.where(column[0] < LAGS, ref, 0.0)
    scale = jnp.sqrt(jnp.sum(ref * ref) / LAGS + 1e-06)
    stacks = (moving / jnp.maximum(counts, 1.0) / scale).astype(jnp.bfloat16)
    back = lax.all_to_all(
        stacks.reshape(days, 1, WIDE), "day", split_axis=0, concat_axis=1, tiled=True
    )
    ref_all = lax.all_gather(ref[None], "day", axis=0, tiled=True)
    return (back[:, :, :LAGS], ref_all[:, :LAGS])


def solution(mesh):
    return jax.shard_map(
        per_device,
        mesh=mesh,
        in_specs=(P("day", "pair", None), P("pair", None), P("day", None)),
        out_specs=(P("day", "pair", None), P("pair", None)),
        check_vma=False,
    )
```

profile of v0, /device:TPU:8, one launch (start us, length us, event | category | flops | bytes accessed | tf_op | source)
XLA Modules:
  0.0 198.5 jit_solution(13838983268094882941)
XLA Ops:
  7.2 0.0 all-gather.3.cloned.1.call-start
  7.2 0.7 all-gather.3.cloned.1.call-update
  7.9 0.8 slice_bitcast_fusion.5
  8.7 0.1 pad_add_fusion
  8.7 0.9 convolution_bitcast_fusion
  9.6 0.1 slice_multiply_fusion
  9.7 0.1 broadcast_in_dim.28
  9.8 37.6 %all-gather.3.cloned.1.call-done = bf16[2,128,4096]{2,1,0:T(8,128)(2,1)} async-done(((bf16[2,16,4096]{2,1,0:T(8,128)(2,1)}), bf16[2,128,4096]{2,1,0:T(8,128)(2,1)}) %all-gather.3.cloned.1.call-update) | async-done | bytes 2097168 | tf_op jit(solution)/shard_map/all_gather | solution.py:33
  47.4 0.0 copy-start
  47.4 1.8 fusion.3
  49.2 0.1 copy-done
  49.3 0.0 copy-start.2
  49.3 0.5 fusion.2
  49.8 0.4 add_convert_fusion
  50.2 2.5 %copy-done.2 = bf16[4096,1024]{1,0:T(8,128)(2,1)S(1)} copy-done((bf16[4096,1024]{1,0:T(8,128)(2,1)S(1)}, bf16[4096,1024]{1,0:T(8,128)(2,1)}, u32[]{:S(2)}) %copy-start.2) | copy-done | bytes 8388632
  52.7 0.0 copy-start.1
  52.7 1.3 fusion.1
  54.0 0.3 copy.12
  54.3 37.4 %all_to_all.33 = bf16[2,64,1024]{2,0,1:T(2,128)(2,1)S(1)} all-to-all(bf16[2,64,1024]{2,0,1:T(2,128)(2,1)S(1)} %copy.12), channel_id=1, replica_groups=mesh['day'=64,'pair'=8] {'day'}, dimensions={1} | all-to-all | bytes 524288 | tf_op jit(solution)/shard_map/all_to_all | solution.py:51
  91.7 0.2 convert_reduce_fusion
  91.9 0.6 broadcast_multiply_fusion
  93.3 0.0 copy-done.1
  93.3 0.2 fusion.18
  93.5 0.2 fusion.11
  93.7 0.1 fusion.9
  93.8 0.5 broadcast.36
  94.3 0.8 reduce.6
  95.1 0.8 reshape.58
  95.9 5.9 %all-to-all-start.1 = ((bf16[64,2,1024]{2,1,0:T(2,128)(2,1)}), bf16[64,2,1024]{2,1,0:T(2,128)(2,1)S(1)}, u32[]{:S(2)}, u32[]{:S(2)}) async-start(bf16[64,2,1024]{2,1,0:T(2,128)(2,1)} %reshape.58), calls=%async_computation.1 | async-start | bytes 524288 | tf_op jit(solution)/shard_map/all_to_all | solution.py:63
  101.9 86.4 %all-gather = f32[64,1,1024]{2,1,0:T(1,128)S(1)} all-gather(f32[1,1,1024]{2,1,0:T(1,128)S(1)} %fusion.15), channel_id=1, replica_groups=mesh['day'=64,'pair'=8] {'day'}, dimensions={0}, use_global_device_ids=true | all-gather | bytes 266240 | tf_op jit(solution)/shard_map/all_gather | solution.py:66
  188.3 0.8 copy.19
  189.1 0.0 all-to-all-done.1
  189.1 0.2 reshape.59
  189.3 1.5 reduce.4
  190.8 0.1 all_to_all.28
  190.9 0.8 copy.15
  (3 shorter events, 0.1 us)
Async XLA Ops:
  7.2 40.2 %all-gather.3.cloned.1.call-start = ((), (), s32[]{:S(2)}) async-start(), calls=%async_computation.2 | async-start | bytes 2359296 | tf_op jit(solution)/shard_map/all_gather | solution.py:33
  47.4 1.9 copy-start
  49.3 3.4 %copy-start.2 = (bf16[4096,1024]{1,0:T(8,128)(2,1)S(1)}, bf16[4096,1024]{1,0:T(8,128)(2,1)}, u32[]{:S(2)}) copy-start(bf16[4096,1024]{1,0:T(8,128)(2,1)} %constant.19.clone) | copy-start | bytes 25165828
  52.7 40.6 %copy-start.1 = (bf16[128,128]{1,0:T(8,128)(2,1)S(1)}, bf16[128,128]{1,0:T(8,128)(2,1)}, u32[]{:S(2)}) copy-start(bf16[128,128]{1,0:T(8,128)(2,1)} %constant.25) | copy-start | bytes 98308
  95.9 93.1 %all-to-all-start.1 = ((bf16[64,2,1024]{2,1,0:T(2,128)(2,1)}), bf16[64,2,1024]{2,1,0:T(2,128)(2,1)S(1)}, u32[]{:S(2)}, u32[]{:S(2)}) async-start(bf16[64,2,1024]{2,1,0:T(2,128)(2,1)} %reshape.58), calls=%async_computation.1 | async-start | bytes 524288 | tf_op jit(solution)/shard_map/all_to_all | solution.py:63
Sparse Core Ops, SparseCore 0:
  10.1 37.1 all-gather.2
where the time goes:
time: 199 us
  blocking collectives  124 us (62%)
  waiting for transfers between devices  38.3 us (19%)
  between operations  14.8 us (7%)
  local copies, waits for them, and re-layouts  6.83 us (3%)
  starting transfers between devices  5.97 us (3%)
  matrix products  4.73 us (2%)
  other arithmetic  4.04 us (2%)
    all_gather x1, blocking collectives, per_device(): ref_all = lax.all_gather(ref[None], 'day', axis=0, tiled=True)  86.4 us
    all_gather x1, waiting for transfers between devices, per_device(): gathered = lax.all_gather(spectra, 'pair', axis=1, tiled=True)  37.6 us
    all_to_all x1, blocking collectives, per_device(): lax.all_to_all(daily, 'day', split_axis=1, concat_axis=0, tiled=True)  37.4 us
    all_to_all x1, starting transfers between devices, per_device(): lax.all_to_all(stacks.reshape(days, 1, WIDE), 'day', split_axis=0, concat...  5.93 us
    unnamed x10, local copies, waits for them, and re-layouts  5.05 us
  transfers between devices with their start and end apart: 2, of which 1 were waited for; matrix products, arithmetic and copies ran while one was open for 1% of the time, Pallas kernels for 0%

commit v1 on v0

--- a/solution.py
+++ b/solution.py
@@ -63,7 +63,9 @@
     back = lax.all_to_all(
         stacks.reshape(days, 1, WIDE), "day", split_axis=0, concat_axis=1, tiled=True
     )
-    ref_all = lax.all_gather(ref[None], "day", axis=0, tiled=True)
+    ref_all = jnp.concatenate(
+        lax.all_to_all(jnp.stack([ref[None]] * lax.axis_size("day")), "day", 0, 0), axis=0
+    )
     return (back[:, :, :LAGS], ref_all[:, :LAGS])
 
 

time: 199 us -> 158 us (0.79)
  blocking collectives: 124 us -> 64.4 us
  waiting for transfers between devices: 38.3 us -> 56.9 us
    all_gather x1 -> x0, blocking collectives: 86.4 us -> none  [per_device(): ref_all = lax.all_gather(ref[None], 'day', axis=0, tiled=True)]
    all_to_all x0 -> x1, blocking collectives: none -> 27 us  [per_device(): lax.all_to_all(stacks.reshape(days, 1, WIDE), 'day', split_axis=0, concat...]
    all_to_all x1, waiting for transfers between devices: 0.01 us -> 18.6 us  [per_device(): lax.all_to_all(jnp.stack([ref[None]] * lax.axis_size('day')), 'day', 0, 0)]
  transfers between devices with their start and end apart: 2 -> 2, of which waited for: 1 -> 2; matrix products, arithmetic and copies ran while one was open for 1% -> 3% of each run, Pallas kernels for 0% -> 0%
where the time goes in v1:
time: 158 us; the launch traced here: 157 us
  blocking collectives  64.4 us (41%)
  waiting for transfers between devices  56.9 us (36%)
  between operations  14.8 us (9%)
  local copies, waits for them, and re-layouts  6.99 us (4%)
  starting transfers between devices  5.56 us (4%)
  matrix products  4.73 us (3%)
  other arithmetic  4.03 us (3%)
    all_gather x1, waiting for transfers between devices, per_device(): gathered = lax.all_gather(spectra, 'pair', axis=1, tiled=True)  37.6 us
    all_to_all x1, blocking collectives, per_device(): lax.all_to_all(daily, 'day', split_axis=1, concat_axis=0, tiled=True)  37.4 us
    all_to_all x1, blocking collectives, per_device(): lax.all_to_all(stacks.reshape(days, 1, WIDE), 'day', split_axis=0, concat...  27 us
    all_to_all x1, waiting for transfers between devices, per_device(): lax.all_to_all(jnp.stack([ref[None]] * lax.axis_size('day')), 'day', 0, 0)  18.6 us
    all_to_all x1, starting transfers between devices, per_device(): lax.all_to_all(jnp.stack([ref[None]] * lax.axis_size('day')), 'day', 0, 0)  5.52 us
    unnamed x10, local copies, waits for them, and re-layouts  4.37 us
  transfers between devices with their start and end apart: 2, of which 2 were waited for; matrix products, arithmetic and copies ran while one was open for 3% of the time, Pallas kernels for 0%

profile of v1, /device:TPU:8, one launch (start us, length us, event | category | flops | bytes accessed | tf_op | source)
XLA Modules:
  0.0 157.4 jit_solution(8390079436361872115)
XLA Ops:
  7.2 0.0 all-gather.2.cloned.1.call-start
  7.2 0.7 all-gather.2.cloned.1.call-update
  7.9 0.8 slice_bitcast_fusion.5
  8.7 0.1 pad_add_fusion
  8.7 0.9 convolution_bitcast_fusion
  9.6 0.1 slice_multiply_fusion
  9.7 0.1 broadcast_in_dim.25
  9.8 37.6 %all-gather.2.cloned.1.call-done = bf16[2,128,4096]{2,1,0:T(8,128)(2,1)} async-done(((bf16[2,16,4096]{2,1,0:T(8,128)(2,1)}), bf16[2,128,4096]{2,1,0:T(8,128)(2,1)}) %all-gather.2.cloned.1.call-update) | async-done | bytes 2097168 | tf_op jit(solution)/shard_map/all_gather | solution.py:33
  47.4 0.0 copy-start
  47.4 1.8 %fusion.3 = f32[128,4096]{1,0:T(8,128)S(1)} fusion(bf16[2,128,4096]{2,1,0:T(8,128)(2,1)} %all-gather.2.cloned.1.call-done, s32[128]{0:T(128)S(1)} %pad_add_fusion), kind=kOutput, calls=%fused_computation.7 | convolution fusion | flops 134234112 | bytes 3146240 | tf_op jit(solution)/shard_map/dot_general | solution.py:36
  49.2 0.1 copy-done
  49.3 0.0 copy-start.2
  49.3 0.5 fusion.2
  49.8 0.4 add_convert_fusion
  50.2 2.5 %copy-done.2 = bf16[4096,1024]{1,0:T(8,128)(2,1)S(1)} copy-done((bf16[4096,1024]{1,0:T(8,128)(2,1)S(1)}, bf16[4096,1024]{1,0:T(8,128)(2,1)}, u32[]{:S(2)}) %copy-start.2) | copy-done | bytes 8388632
  52.7 0.0 copy-start.1
  52.7 1.3 fusion.1
  54.0 0.3 copy.12
  54.3 37.4 %all_to_all.38 = bf16[2,64,1024]{2,0,1:T(2,128)(2,1)S(1)} all-to-all(bf16[2,64,1024]{2,0,1:T(2,128)(2,1)S(1)} %copy.12), channel_id=1, replica_groups=mesh['day'=64,'pair'=8] {'day'}, dimensions={1} | all-to-all | bytes 524288 | tf_op jit(solution)/shard_map/all_to_all | solution.py:51
  91.7 0.2 convert_reduce_fusion
  91.9 0.6 multiply_select_fusion
  93.3 0.0 copy-done.1
  93.3 0.2 fusion.17
  93.5 0.2 fusion.11
  93.7 0.1 fusion.9
  93.8 0.5 broadcast.30
  94.3 0.8 reduce.6
  95.1 0.1 reshape.53
  95.2 27.0 %all_to_all.39 = bf16[64,2,1024]{2,1,0:T(2,128)(2,1)S(1)} all-to-all(bf16[64,2,1024]{2,1,0:T(2,128)(2,1)S(1)} %reshape.53), channel_id=1, replica_groups=mesh['day'=64,'pair'=8] {'day'}, dimensions={0} | all-to-all | bytes 524288 | tf_op jit(solution)/shard_map/all_to_all | solution.py:63
  122.2 0.8 stack.3
  123.1 5.5 %all-to-all-start.2 = ((f32[64,1,1024]{2,1,0:T(1,128)}), f32[64,1,1024]{2,1,0:T(1,128)S(1)}, u32[]{:S(2)}, u32[]{:S(2)}) async-start(f32[64,1,1024]{2,1,0:T(1,128)} %stack.3), calls=%async_computation.2 | async-start | bytes 524288 | tf_op jit(solution)/shard_map/all_to_all | solution.py:67
  128.6 0.2 reshape.54
  128.9 1.5 reduce.4
  130.4 0.1 all_to_all.31
  130.5 0.8 copy.15
  131.2 18.6 %all-to-all-done.2 = f32[64,1,1024]{2,1,0:T(1,128)S(1)} async-done(((f32[64,1,1024]{2,1,0:T(1,128)}), f32[64,1,1024]{2,1,0:T(1,128)S(1)}, u32[]{:S(2)}, u32[]{:S(2)}) %all-to-all-start.2) | async-done | bytes 262176 | tf_op jit(solution)/shard_map/all_to_all | solution.py:67
  149.8 0.8 copy.19
  (2 shorter events, 0.1 us)
Async XLA Ops:
  7.2 40.2 %all-gather.2.cloned.1.call-start = ((), (), s32[]{:S(2)}) async-start(), calls=%async_computation.3 | async-start | bytes 2359296 | tf_op jit(solution)/shard_map/all_gather | solution.py:33
  47.4 1.9 %copy-start = (bf16[2,128,4096]{2,1,0:T(8,128)(2,1)S(1)}, bf16[2,128,4096]{2,1,0:T(8,128)(2,1)}, u32[]{:S(2)}) copy-start(bf16[2,128,4096]{2,1,0:T(8,128)(2,1)} %all-gather.2.cloned.1.call-done) | copy-start | bytes 6291460
  49.3 3.4 %copy-start.2 = (bf16[4096,1024]{1,0:T(8,128)(2,1)S(1)}, bf16[4096,1024]{1,0:T(8,128)(2,1)}, u32[]{:S(2)}) copy-start(bf16[4096,1024]{1,0:T(8,128)(2,1)} %constant.19.clone) | copy-start | bytes 25165828
  52.7 40.6 %copy-start.1 = (bf16[128,128]{1,0:T(8,128)(2,1)S(1)}, bf16[128,128]{1,0:T(8,128)(2,1)}, u32[]{:S(2)}) copy-start(bf16[128,128]{1,0:T(8,128)(2,1)} %constant.25) | copy-start | bytes 98308
  123.1 26.8 %all-to-all-start.2 = ((f32[64,1,1024]{2,1,0:T(1,128)}), f32[64,1,1024]{2,1,0:T(1,128)S(1)}, u32[]{:S(2)}, u32[]{:S(2)}) async-start(f32[64,1,1024]{2,1,0:T(1,128)} %stack.3), calls=%async_computation.2 | async-start | bytes 524288 | tf_op jit(solution)/shard_map/all_to_all | solution.py:67
Sparse Core Ops, SparseCore 0:
  10.1 37.1 all-gather.1
